TPU v7x, 32 devices: a whole 2x2x4 slice. The times are simulated.
32 devices in a mesh: row: 8 (over z, core), col: 4 (over y, x).
Axes of the slice: x: 2, y: 2, z: 4, core: 2. Of those that a mesh axis runs over, the one named last changes fastest.
Arguments:
- stored: bfloat16 [1024, 51200], P(('row', 'col')), may hold values from -6 to 6
- integrals: bfloat16 [51200, 25600], P('row', 'col'), may hold values from -0.02734375 to 0.02734375
- layout: int32 [1024], replicated, may hold values from 0 to 1023, each once
- partner: int32 [1024], replicated, may hold values from 0 to 1023, as said below
Outputs:
- residual_out: bfloat16 [1024, 25600], P('row', 'col')
Inputs may be any that keep to these rules, and one draw needn't show every extreme that they name: partner is an involution without fixed points: partner[p] != p and partner[partner[p]] = p. `layout`: each slab pair stands in exactly one stored row.
All inputs are finite; a program needn't handle non-finite values.
Results may differ from a plain program's by a relative error of at most 0.001.
Values may be sent and summed in bfloat16 or wider, within the bound.
No kernel may reach another device: no remote copies, remote signals or barrier semaphores. Data moves between devices by JAX's collectives and lax.ppermute only.
A program may use at most 256 MiB of HBM per device.

v0:
```python
import jax
import jax.numpy as jnp
from jax import lax
from jax.sharding import PartitionSpec as P


def per_device(stored, integrals, layout, partner):
    local_rows = stored.shape[0]
    n_row = lax.axis_size("row")
    n_col = lax.axis_size("col")
    total = local_rows * n_row * n_col
    regrouped = lax.all_to_all(stored, "row", split_axis=1, concat_axis=0, tiled=True)
    partial_sums = jnp.dot(
        lax.all_gather(regrouped, "col", axis=0, tiled=True),
        integrals,
        preferred_element_type=jnp.float32,
    )
    place = jnp.arange(total, dtype=jnp.int32)
    group_size = n_row * local_rows
    source_col = place // group_size
    remain = place % group_size
    source_row = remain // local_rows
    offset = remain % local_rows
    stored_index = (source_row * n_col + source_col) * local_rows + offset
    where_global = jnp.zeros((total,), jnp.int32).at[layout[stored_index]].set(place)
    difference = partial_sums[where_global] - partial_sums[where_global[partner]]
    return lax.psum_scatter(difference, "row", scatter_dimension=0, tiled=True).astype(jnp.bfloat16)


def solution(mesh):
    return jax.shard_map(
        per_device,
        mesh=mesh,
        in_specs=(P(("row", "col"), None), P("row", "col"), P(), P()),
        out_specs=P("row", "col"),
        check_vma=False,
    )
```

profile of v0, /device:TPU:0, one launch (start us, length us, event | category | flops | bytes accessed | tf_op | source)
XLA Modules:
  0.0 667.0 jit_solution(2885701985231506991)
XLA Ops:
  6.5 0.0 copy-start
  6.5 0.0 all-gather.2.cloned.1.call-start
  6.5 2.2 copy.9
  8.7 80.6 %all_to_all.19 = bf16[32,8,6400]{2,0,1:T(8,128)(2,1)} all-to-all(bf16[32,8,6400]{2,0,1:T(8,128)(2,1)S(1)} %bitcast.16), channel_id=1, replica_groups=mesh['row'=8,'col'=4] {'row'}, dimensions={1} | all-to-all | bytes 6553600 | tf_op jit(solution)/shard_map/all_to_all | solution.py:12
  89.3 0.0 all-gather.2.cloned.1.call-update
  89.3 0.0 reduce-scatter.2.cloned.1.call-start
  89.4 0.0 copy-done
  89.4 4.5 gather_fusion
  94.0 4.3 scatter_custom_fusion
  98.3 0.7 fusion.4
  99.0 4.5 gather_fusion.2
  103.5 0.6 fusion.3
  104.1 0.6 broadcast_clamp_fusion
  104.7 110.5 %all-gather.2.cloned.1.call-done = bf16[1024,6400]{1,0:T(8,128)(2,1)} async-done(((bf16[256,6400]{1,0:T(8,128)(2,1)}), bf16[1024,6400]{1,0:T(8,128)(2,1)}) %all-gather.2.cloned.1.call-update) | async-done | bytes 13107216 | tf_op jit(solution)/shard_map/all_gather | solution.py:14
  215.3 97.6 %fusion.7 = f32[1024,6400]{1,0:T(8,128)} fusion(bf16[1024,6400]{1,0:T(8,128)(2,1)} %all-gather.2.cloned.1.call-done, bf16[6400,6400]{1,0:T(8,128)(2,1)} %param.5), kind=kOutput, calls=%fused_computation.30 | convolution fusion | flops 83886080000 | bytes 121241600 | tf_op jit(solution)/shard_map/dot_general | solution.py:13
  312.9 0.0 copy-done.3
  312.9 30.1 %gather_fusion.3 = f32[1024,6400]{1,0:T(8,128)} fusion(f32[1024,6400]{1,0:T(8,128)} %fusion.7, s32[1024]{0:T(1024)S(1)} %copy-done.3), kind=kCustom, calls=%fused_computation.3 | custom fusion | bytes 52432896 | tf_op jit(solution)/shard_map/gather | solution.py:26
  343.0 0.0 copy-done.2
  343.0 30.1 %gather_fusion.1 = f32[1024,6400]{1,0:T(8,128)} fusion(f32[1024,6400]{1,0:T(8,128)} %fusion.7, s32[1024]{0:T(1024)S(1)} %copy-done.2), kind=kCustom, calls=%fused_computation.1 | custom fusion | bytes 52432896 | tf_op jit(solution)/shard_map/gather | solution.py:26
  373.1 26.6 %sub.15 = f32[1024,6400]{1,0:T(8,128)} subtract(f32[1024,6400]{1,0:T(8,128)} %gather_fusion.1, f32[1024,6400]{1,0:T(8,128)} %gather_fusion.3) | non-fusion elementwise | flops 6553600 | bytes 78643200 | tf_op jit(solution)/shard_map/sub | solution.py:26
  399.7 0.0 reduce-scatter.2.cloned.1.call-update
  399.7 257.2 %reduce-scatter.2.cloned.1.call-done = f32[128,6400]{1,0:T(8,128)} async-done(((f32[1024,6400]{1,0:T(8,128)}), f32[128,6400]{1,0:T(8,128)}) %reduce-scatter.2.cloned.1.call-update) | async-done | bytes 3276816 | tf_op jit(solution)/shard_map/reduce_scatter | solution.py:27
  656.9 3.3 convert_element_type.3
  660.2 0.0 copy-done.1
  (8 shorter events, 0.1 us)
Async XLA Ops:
  6.5 82.9 %copy-start = (s32[1024]{0:T(1024)S(1)}, s32[1024]{0:T(1024)}, u32[]{:S(2)}) copy-start(s32[1024]{0:T(1024)} %param.6) | copy-start | bytes 12292
  6.5 208.7 %all-gather.2.cloned.1.call-start = ((), (), s32[]{:S(2)}) async-start(), calls=%async_computation.2 | async-start | bytes 16384000 | tf_op jit(solution)/shard_map/all_gather | solution.py:14
  89.3 567.6 %reduce-scatter.2.cloned.1.call-start = ((), (), s32[]{:S(2)}) async-start(), calls=%async_computation.3 | async-start | bytes 29491200 | tf_op jit(solution)/shard_map/reduce_scatter | solution.py:27
  215.3 97.6 %copy-start.3 = (s32[1024]{0:T(1024)S(1)}, s32[1024]{0:T(1024)}, u32[]{:S(2)}) copy-start(s32[1024]{0:T(1024)} %broadcast_clamp_fusion) | copy-start | bytes 12292
  312.9 30.1 %copy-start.2 = (s32[1024]{0:T(1024)S(1)}, s32[1024]{0:T(1024)}, u32[]{:S(2)}) copy-start(s32[1024]{0:T(1024)} %fusion.3) | copy-start | bytes 12292
  373.1 287.1 %copy-start.1 = (s32[1024]{0:T(1024)S(1)}, s32[1024]{0:T(1024)}, u32[]{:S(2)}) copy-start(s32[1024]{0:T(1024)} %param.6) | copy-start | bytes 12292
Sparse Core Ops, SparseCore 0:
  89.4 125.7 all-gather.1
  399.9 257.0 reduce-scatter.1
where the time goes:
time: 667 us
  waiting for transfers between devices  368 us (55%)
  matrix products  97.6 us (15%)
  blocking collectives  80.6 us (12%)
  local copies, waits for them, and re-layouts  75.8 us (11%)
  other arithmetic  31.8 us (5%)
  between operations  13.5 us (2%)
    reduce_scatter x1, waiting for transfers between devices, per_device(): lax.psum_scatter(difference, 'row', scatter_dimension=0, tiled=True)  257 us
    all_gather x1, waiting for transfers between devices, per_device(): lax.all_gather(regrouped, 'col', axis=0, tiled=True)  111 us
    dot_general x1, matrix products, per_device(): jnp.dot(lax.all_gather(regrouped, 'col', axis=0, tiled=True), integrals,...  97.6 us
    all_to_all x1, blocking collectives, per_device(): lax.all_to_all(stored, 'row', split_axis=1, concat_axis=0, tiled=True)  80.6 us
    gather x1, local copies, waits for them, and re-layouts, per_device(): partial_sums[where_global] - partial_sums[where_global[partner]]  30.1 us
    gather x1, local copies, waits for them, and re-layouts, per_device(): partial_sums[where_global[partner]]  30.1 us
    sub x1, other arithmetic, per_device(): partial_sums[where_global] - partial_sums[where_global[partner]]  26.6 us
  transfers between devices with their start and end apart: 2, of which 2 were waited for; matrix products, arithmetic and copies ran while one was open for 2% of the time, Pallas kernels for 0%

commit v1 on v0

v1 whole, which is shorter than its diff:
```python
import functools

import jax
import jax.numpy as jnp
import numpy as np
from jax import lax
from jax.experimental import pallas as pl
from jax.experimental.pallas import tpu as pltpu
from jax.sharding import PartitionSpec as P

F32, BF16, F8, I16, I32 = jnp.float32, jnp.bfloat16, jnp.float8_e4m3fn, jnp.int16, jnp.int32
UNITS = 25
CHUNKS = (6, 9, 10)
WIDE = 5
GROUPS = (2, 3)
PARTS = ((0, 0, 5), (0, 5, 5), (1, 0, 5), (1, 5, 5), (1, 10, 5))
EXTRA = 16
MIB = 1024 * 1024
COST = 1
ORDER = (
    (0, 0), (1, 0), (2, 0), (0, 1), (3, 0), (2, 1), (1, 1), (2, 2), (2, 3), (3, 1), (2, 4), (4, 0), (3, 2), (5, 0), (4, 1),
    (3, 3), (5, 1), (4, 2), (3, 4), (5, 2), (4, 3), (5, 3), (4, 4), (5, 4),
)


def in_place(ref_rows, width):
    return pl.BlockSpec((ref_rows, width), lambda n, *_: (0, n))


class Chain:
    def __init__(self):
        self.mark = None

    def call(
        self, body, arrays, in_specs, out_specs, out_shape, grid, scalars=None, vmem=16, cost=COST, scratch_shapes=(), **kw
    ):
        marks = [] if self.mark is None else [self.mark]
        n_scalars, n_in, n_out, n_marks = scalars is not None, len(arrays), len(out_shape), len(marks)

        def wrapped(*refs):
            ahead, rest = refs[:n_scalars], refs[n_scalars:]
            outs, scratch = rest[n_in + n_marks :][:n_out], rest[n_in + n_marks + n_out + 1 :]
            body(*ahead, *rest[:n_in], *outs, *scratch)
            mark = rest[n_in + n_marks + n_out]
            mark[...] = jnp.zeros_like(mark)

        anywhere = pl.BlockSpec(memory_space=pl.ANY)
        *outs, self.mark = pl.pallas_call(
            wrapped,
            grid_spec=pltpu.PrefetchScalarGridSpec(
                num_scalar_prefetch=n_scalars,
                grid=grid,
                in_specs=[*in_specs, *[anywhere] * n_marks],
                out_specs=[*out_specs, pl.BlockSpec((8, 128), lambda *_: (0, 0))],
                scratch_shapes=scratch_shapes,
            ),
            out_shape=[*out_shape, jax.ShapeDtypeStruct((8, 128), F32)],
            compiler_params=pltpu.CompilerParams(vmem_limit_bytes=vmem * MIB),
            cost_estimate=pl.CostEstimate(flops=cost, bytes_accessed=cost, transcendentals=0),
            **kw,
        )(*([scalars] if n_scalars else []), *arrays, *marks)
        return outs


def split_body(place_ref, *refs):
    for i, ref in enumerate(refs[:-1]):
        refs[-1][i] = ref[...]


def join_body(*refs):
    count = len(refs) // 3
    for i in range(count):
        rows = refs[2 * i].shape[0]
        refs[2 * count + i][0:rows, :] = refs[2 * i][...]
        refs[2 * count + i][rows:, :] = refs[2 * i + 1][...]


def stack_body(line, with_halves, with_pieces):
    def body(place_ref, *refs):
        refs = list(refs)
        pieces = [refs.pop(0) for _ in range(line * with_halves)]
        own = [refs.pop(0) for _ in range(line * with_pieces)]
        other = [refs.pop(0) for _ in range(line * with_pieces)]
        halves = [refs.pop(0) for _ in range(2 * with_halves)]
        for i, ref in enumerate(pieces):
            rows, at = ref.shape[0], i % (line // 2)
            halves[i // (line // 2)][at * rows : (at + 1) * rows, :] = ref[...]
        for first, second, target in zip(own, other, refs):
            rows = first.shape[0]
            target[0:rows, :] = first[...]
            target[rows:, :] = second[...]

    return body


def pair_rows_body(select_ref, *refs):
    *piece_refs, high_ref, low_ref, scale_ref = refs
    at = pl.program_id(0)

    @pl.when(at == 0)
    def _():
        tops = [jnp.max(jnp.abs(ref[...]), axis=0, keepdims=True) for ref in piece_refs]
        top = jnp.max(functools.reduce(jnp.maximum, tops).astype(F32), axis=1, keepdims=True)
        scale_ref[...] = jnp.broadcast_to(jnp.maximum(top, 1e-30) * (2.0**-7 / 440.0), scale_ref.shape)

    width = high_ref.shape[1]
    here = pl.ds(pl.multiple_of(at * width, width), width)
    rows = jnp.concatenate([ref[:, here] for ref in piece_refs], axis=0)
    diff = jnp.dot(select_ref[...], rows, preferred_element_type=F32)
    high = diff.astype(BF16)
    high_ref[...] = high
    low_ref[...] = ((diff - high.astype(F32)) * (1.0 / scale_ref[0:1, 0:1])).astype(F8)


def product(high_ref, low_ref, scale_ref, block_ref):
    block = block_ref[...]
    value = jnp.dot(high_ref[...], block, preferred_element_type=F32)
    top = jnp.maximum(jnp.max(jnp.abs(block), axis=0, keepdims=True).astype(F32), 1e-30)
    small = (block * (440.0 / top).astype(BF16)).astype(F8)
    low = jnp.dot(low_ref[...], small, preferred_element_type=F32)
    return value + low * scale_ref[0:1, 0:1] * (1.0 / (440.0 / top).astype(BF16).astype(F32))


def first_body(high_ref, low_ref, scale_ref, block_ref, out_ref):
    out_ref[...] = product(high_ref, low_ref, scale_ref, block_ref)


def middle_body(high_ref, low_ref, scale_ref, block_ref, sum_ref, out_ref):
    out_ref[...] = sum_ref[...] + product(high_ref, low_ref, scale_ref, block_ref)


def last_body(high_ref, low_ref, scale_ref, block_ref, sum_ref, own_ref, other_ref):
    value = sum_ref[...] + product(high_ref, low_ref, scale_ref, block_ref)
    half = value.shape[0] // 2
    own_ref[...] = value[:half]
    other_ref[...] = value[half:]


def encode(value, out_ref):
    rows = value.shape[0]
    top = jnp.maximum(jnp.max(jnp.abs(value), axis=0, keepdims=True), 1e-30)
    step = jnp.ceil(16.0 * jnp.log2(top * (1.0 / 32700.0)))
    inverse = jnp.exp2(step * (-1.0 / 16.0))
    fixed = jnp.clip(jnp.round(value * inverse), -32767.0, 32767.0)
    out_ref[0:rows, :] = fixed.astype(I32).astype(I16)
    out_ref[rows:, :] = jnp.broadcast_to(step, (EXTRA, value.shape[1])).astype(I32).astype(I16)


def decode(ref):
    rows = ref.shape[0] - EXTRA
    step = ref[rows:, :].astype(I32).astype(F32)[0:1, :]
    return ref[0:rows, :].astype(I32).astype(F32) * jnp.exp2(step * (1.0 / 16.0))


def add_plain_body(a_ref, b_ref, sum_ref, code_ref):
    value = a_ref[...] + b_ref[...]
    sum_ref[...] = value
    encode(value, code_ref)


def add_coded_body(a_ref, code_in_ref, sum_ref, code_ref):
    value = a_ref[...] + decode(code_in_ref)
    sum_ref[...] = value
    encode(value, code_ref)


def add_last_body(a_ref, code_in_ref, out_ref):
    out_ref[...] = (a_ref[...] + decode(code_in_ref)).astype(BF16)


def pick_body(pick_ref, own_ref, other_ref, out_ref, far_ref):
    half = own_ref.shape[0]
    near = out_ref.shape[0]
    value = jnp.dot(pick_ref[:, 0:half], own_ref[...], preferred_element_type=F32)
    value += jnp.dot(pick_ref[:, half:], other_ref[...], preferred_element_type=F32)
    out_ref[...] = value[:near].astype(BF16)
    far_ref[...] = value[near:].astype(BF16)


def per_device(stored, integrals, layout, partner):
    rows = stored.shape[0]
    n_row, n_col = lax.axis_size("row"), lax.axis_size("col")
    line = n_row // 2
    total = rows * n_row * n_col
    pairs = total // 2
    half = pairs // 2
    depth, columns = integrals.shape
    unit, tile = depth // UNITS, columns // UNITS
    r, c = lax.axis_index("row"), lax.axis_index("col")
    z, core = r // 2, r % 2
    place = jnp.stack([z, core]).astype(I32)
    siblings = [(i, i ^ 1) for i in range(n_row)]
    chain = Chain()
    starts = [sum(CHUNKS[:i]) for i in range(len(CHUNKS))]

    def split():
        def at(i):
            return lambda u, p: (0, 2 * i + 1 - p[1])

        return chain.call(
            split_body,
            [stored] * line,
            [pl.BlockSpec((rows, depth), at(i)) for i in range(line)],
            [pl.BlockSpec((line, rows, depth), lambda u, p: (0, 0, 0))],
            [jax.ShapeDtypeStruct((line, rows, depth), BF16)],
            (1,),
            scalars=place,
        )[0]

    def stack(pieces, following):
        def whole(shape):
            return pl.BlockSpec(shape, lambda u, p: (0, 0))

        def at(step):
            return lambda u, p: (0, ((2 * lax.rem(p[0] + step, line) + p[1]) * UNITS + starts[following]) * unit)

        def other_at(step):
            return lambda u, p: (lax.rem(p[0] + step, line), 0, starts[following] * unit)

        arrays, in_specs, shapes = [], [], []
        if pieces is not None:
            rows_of, width = pieces[0].shape
            arrays += pieces
            in_specs += [whole((rows_of, width))] * line
            shapes += [(rows_of * line // 2, width)] * 2
        if following is not None:
            width = CHUNKS[following] * unit
            arrays += [stored] * line + [others] * line
            in_specs += [pl.BlockSpec((pl.Element(rows), pl.Element(width)), at(s)) for s in range(line)]
            in_specs += [pl.BlockSpec((None, pl.Element(rows), pl.Element(width)), other_at(s)) for s in range(line)]
            shapes += [(2 * rows, width)] * line
        outs = chain.call(
            stack_body(line, pieces is not None, following is not None),
            arrays,
            in_specs,
            [whole(shape) for shape in shapes],
            [jax.ShapeDtypeStruct(shape, BF16) for shape in shapes],
            (1,),
            scalars=place,
        )
        halves = outs[:2] if pieces is not None else None
        return halves, outs[2 if pieces is not None else 0 :]

    def along_z(pieces):
        out = pieces[:1]
        for step in range(1, line):
            perm = [(2 * i + k, 2 * ((i + step) % line) + k) for i in range(line) for k in range(2)]
            out.append(lax.ppermute(pieces[step], "row", perm))
        return out

    bits = [1 << b for b in range(n_col.bit_length() - 1)]
    orders = [bits, bits[::-1]]

    def over_col(halves):
        have = [[h] for h in halves]
        joined = halves
        for i in range(len(bits)):
            if i:
                width = joined[0].shape[1]
                grown = 2 * joined[0].shape[0]
                specs = [pl.BlockSpec((grown // 2, width), lambda u: (0, 0))] * 4
                joined = chain.call(
                    join_body,
                    [x for h in range(2) for x in (joined[h], have[h][-1])],
                    specs,
                    [pl.BlockSpec((grown, width), lambda u: (0, 0))] * 2,
                    [jax.ShapeDtypeStruct((grown, width), BF16)] * 2,
                    (1,),
                    vmem=32,
                )
            for h in range(2):
                perm = [(x, x ^ orders[h][i]) for x in range(n_col)]
                have[h].append(lax.ppermute(joined[h], "col", perm))
            yield
        return have[0] + have[1]

    def pair_rows(chunk, pieces):
        width = CHUNKS[chunk] * unit
        shapes = [((pairs, width), BF16), ((pairs, width), F8), ((8, 128), F32)]
        return chain.call(
            pair_rows_body,
            [select, *pieces],
            [pl.BlockSpec((pairs, total), lambda n: (0, 0))] + [pl.BlockSpec(p.shape, lambda n: (0, 0)) for p in pieces],
            [in_place(pairs, unit), in_place(pairs, unit), pl.BlockSpec((8, 128), lambda n: (0, 0))],
            [jax.ShapeDtypeStruct(shape, kind) for shape, kind in shapes],
            (CHUNKS[chunk],),
            vmem=32,
        )

    wide = WIDE * tile

    def product_specs(chunk, diff, first):
        rows_of = CHUNKS[chunk] * unit
        return [
            *[pl.BlockSpec(d.shape, lambda n: (0, 0)) for d in diff],
            pl.BlockSpec(
                (pl.Element(rows_of), pl.Element(wide)), lambda n: (starts[chunk] * unit, (first + n) * wide)
            ),
        ]

    def accumulate(chunk, diff, sums):
        in_specs = product_specs(chunk, diff, 0)
        kw = dict(
            out_specs=[in_place(pairs, wide)],
            out_shape=[jax.ShapeDtypeStruct((pairs, columns), F32)],
            grid=(columns // wide,),
            vmem=56,
        )
        if sums is None:
            return chain.call(first_body, [*diff, integrals], in_specs, **kw)[0]
        return chain.call(
            middle_body,
            [*diff, integrals, sums],
            [*in_specs, in_place(pairs, wide)],
            input_output_aliases={4: 0},
            **kw,
        )[0]

    def finish(group, diff, sums):
        first = sum(GROUPS[:group])
        return chain.call(
            last_body,
            [*diff, integrals, sums],
            [*product_specs(n - 1, diff, first), pl.BlockSpec((pairs, wide), lambda n: (0, first + n))],
            [in_place(half, wide)] * 2,
            [jax.ShapeDtypeStruct((half, GROUPS[group] * wide), F32)] * 2,
            (GROUPS[group],),
            vmem=56,
        )

    def by_columns(body, arrays, outs, first=0, units=None):
        count = arrays[-1].shape[1] // tile if units is None else units
        return chain.call(
            body,
            arrays,
            [pl.BlockSpec((a.shape[0], tile), lambda n: (0, first + n)) for a in arrays],
            [in_place(rows_of, tile) for rows_of, _ in outs],
            [jax.ShapeDtypeStruct((rows_of, count * tile), kind) for rows_of, kind in outs],
            (count,),
        )

    def row_ids():
        entries = []
        for h in range(2):
            masks = [0]
            for bit in orders[h]:
                masks += [m ^ bit for m in masks]
            for m in masks:
                for step in range(h * line // 2, (h + 1) * line // 2):
                    for flip in range(2):
                        entries += [(m, step, flip, offset) for offset in range(rows)]
        mask, step, flip, offset = np.array(entries, np.int32).T
        return ((2 * ((z - step) % line) + (core ^ flip)) * n_col + (c ^ mask)) * rows + offset

    n = len(CHUNKS)
    others = lax.ppermute(split(), "row", siblings)
    _, pieces = stack(None, 0)
    pieces = along_z(pieces)

    slab = jnp.arange(total, dtype=I32) + chain.mark[0, 0].astype(I32)
    is_first = slab < partner
    before = is_first[None, :] & (slab[None, :] < jnp.minimum(slab, partner)[:, None])
    number = jnp.sum(before.astype(I32), axis=1) + 1
    signed = jnp.where(is_first, number, -number)
    held = jnp.sum(jnp.where(slab[None, :] == layout[:, None], signed[None, :], 0), axis=1)
    held = jnp.sum(jnp.where(slab[None, :] == row_ids()[:, None], held[None, :], 0), axis=1)
    order = (jnp.arange(pairs, dtype=I32) + core * half) % pairs + 1
    select = (order[:, None] == held[None, :]).astype(BF16) - (order[:, None] == -held[None, :]).astype(BF16)
    middle = line // 2
    mine_rows = total // n_row
    outward = jnp.where(z < middle, -1, 1)
    owners = jnp.clip(z + outward * np.arange(middle, dtype=np.int32), 0, line - 1)
    wanted = (2 * jnp.repeat(owners, mine_rows) + core) * mine_rows + np.tile(np.arange(mine_rows, dtype=np.int32), middle)
    mine = jnp.sum(jnp.where(slab[None, :] == wanted[:, None], signed[None, :], 0), axis=1)
    pick = (mine[:, None] == order[None, :]).astype(BF16) - (mine[:, None] == -order[None, :]).astype(BF16)

    sums = None

    def advance(exchange):
        try:
            next(exchange)
        except StopIteration as end:
            return end.value

    halves, pieces = stack(pieces, 1)
    pieces = along_z(pieces)
    exchange = over_col(halves)
    blocks = None
    while blocks is None:
        blocks = advance(exchange)
    for i in range(1, n):
        halves, pieces = following if i > 1 else stack(pieces, i + 1 if i + 1 < n else None)
        if i + 1 < n:
            pieces = along_z(pieces)
        exchange = over_col(halves)
        advance(exchange)
        diff = pair_rows(i - 1, blocks)
        blocks = None
        while blocks is None:
            blocks = advance(exchange)
        sums = accumulate(i - 1, diff, sums)
        if i + 1 < n:
            following = stack(pieces, i + 2 if i + 2 < n else None)
    diff = pair_rows(n - 1, blocks)

    def along(pairs_of_z):
        return [(2 * a + k, 2 * b + k) for a, b in pairs_of_z for k in range(2)]

    groups = [None] * len(GROUPS)

    def send(group):
        own, foreign = groups[group]
        anywhere = pl.BlockSpec(memory_space=pl.ANY)
        shape = jax.ShapeDtypeStruct(foreign.shape, foreign.dtype)
        (foreign,) = chain.call(
            lambda *refs: None, [foreign], [anywhere], [anywhere], [shape], (1,), input_output_aliases={0: 0}
        )
        groups[group] = [own, lax.ppermute(foreign, "row", siblings)]

    def begin(part):
        group, first, units = PARTS[part]
        return groups[group], first, units

    def inward(step, state):
        outs = [(half, F32), (half + EXTRA, I16)]
        if step == 0:
            value, code = by_columns(add_plain_body, state[0], outs, state[1], state[2])
        else:
            value, code = by_columns(add_coded_body, list(state), outs)
        if step < middle - 1:
            perm = along([(step, step + 1), (line - 1 - step, line - 2 - step)])
        else:
            perm = along([(middle - 1, middle), (middle, middle - 1)])
        return value, lax.ppermute(code, "row", perm)

    def whole(state):
        (done,) = by_columns(add_last_body, list(state), [(half, BF16)])
        return done, lax.ppermute(done, "row", siblings)

    def spread(state):
        width = state[0].shape[1]
        far = (middle - 1) * mine_rows
        own, rest = chain.call(
            pick_body,
            [pick, *state],
            [pl.BlockSpec(pick.shape, lambda n: (0, 0)), in_place(half, tile), in_place(half, tile)],
            [in_place(mine_rows, tile), in_place(far, tile)],
            [jax.ShapeDtypeStruct((mine_rows, width), BF16), jax.ShapeDtypeStruct((far, width), BF16)],
            (width // tile,),
        )
        distance = jnp.where(z < middle, middle - 1 - z, z - middle)
        for step in range(middle - 1):
            perm = along([(middle - 1 - step, middle - 2 - step), (middle + step, middle + 1 + step)])
            rest = lax.ppermute(rest, "row", perm)
            own = jnp.where(distance == step + 1, rest[:mine_rows], own)
            rest = rest[mine_rows:]
        return own

    stages = [lambda s, k=k: inward(k, s) for k in range(middle)] + [whole, spread]
    state = [None] * len(PARTS)
    for stage, item in ORDER if len(stages) == 4 else (
        [(k, g) for k in (0, 1) for g in range(len(GROUPS))]
        + sorted(
            ((k + 2, p) for p in range(len(PARTS)) for k in range(len(stages))), key=lambda x: (x[0] + x[1], x[0])
        )
    ):
        if stage == 0:
            groups[item] = finish(item, diff, sums)
        elif stage == 1:
            send(item)
        else:
            state[item] = stages[stage - 2](begin(item) if stage == 2 else state[item])
    return jnp.concatenate(state, axis=1)


def solution(mesh):
    return jax.shard_map(
        per_device,
        mesh=mesh,
        in_specs=(P(("row", "col"), None), P("row", "col"), P(), P()),
        out_specs=P("row", "col"),
        check_vma=False,
    )
```

time: 667 us -> 354 us (0.53)
  waiting for transfers between devices: 368 us -> 84.5 us
  Pallas kernels: 0 us -> 159 us
  matrix products: 97.6 us -> 0 us
  blocking collectives: 80.6 us -> 0 us
  starting transfers between devices: 0.04 us -> 76.8 us
  local copies, waits for them, and re-layouts: 75.8 us -> 26.1 us
  other arithmetic: 31.8 us -> 5.04 us
  between operations: 13.5 us -> 1.38 us
    reduce_scatter x1 -> x0, waiting for transfers between devices: 257 us -> none  [per_device(): lax.psum_scatter(difference, 'row', scatter_dimension=0, tiled=True)]
    pallas_call x0 -> x37, Pallas kernels: none -> 159 us  [call(): pl.pallas_call(wrapped, grid_spec=pltpu.PrefetchScalarGridSpec(num_scalar...]
    all_gather x1 -> x0, waiting for transfers between devices: 111 us -> none  [per_device(): lax.all_gather(regrouped, 'col', axis=0, tiled=True)]
    dot_general x1 -> x0, matrix products: 97.6 us -> none  [per_device(): jnp.dot(lax.all_gather(regrouped, 'col', axis=0, tiled=True), integrals,...]
    ppermute x0 -> x44, waiting for transfers between devices: none -> 84.5 us  [the longest x5 24.2 us: spread(): rest = lax.ppermute(rest, 'row', perm)]
    all_to_all x1 -> x0, blocking collectives: 80.6 us -> none  [per_device(): lax.all_to_all(stored, 'row', split_axis=1, concat_axis=0, tiled=True)]
    ppermute x0 -> x44, starting transfers between devices: none -> 76.8 us  [the longest x10 32.3 us: inward(): return (value, lax.ppermute(code, 'row', perm))]
    gather x4 -> x0, local copies, waits for them, and re-layouts: 69.3 us -> none  [the longest x1 30.1 us: per_device(): partial_sums[where_global] - partial_sums[where_global[partner]]]
  transfers between devices with their start and end apart: 2 -> 44, of which waited for: 2 -> 19; matrix products, arithmetic and copies ran while one was open for 2% -> 1% of each run, Pallas kernels for 0% -> 34%
where the time goes in v1:
time: 354 us; the launch traced here: 353 us
  Pallas kernels  159 us (45%)
  waiting for transfers between devices  84.5 us (24%)
  starting transfers between devices  76.8 us (22%)
  local copies, waits for them, and re-layouts  26.1 us (7%)
  other arithmetic  5.04 us (1%)
    pallas_call x37, Pallas kernels, call(): pl.pallas_call(wrapped, grid_spec=pltpu.PrefetchScalarGridSpec(num_scalar...  159 us
    ppermute x10, starting transfers between devices, inward(): return (value, lax.ppermute(code, 'row', perm))  32.3 us
    unnamed x96, local copies, waits for them, and re-layouts  25.6 us
    ppermute x5, waiting for transfers between devices, spread(): rest = lax.ppermute(rest, 'row', perm)  24.2 us
    ppermute x9, waiting for transfers between devices, along_z(): out.append(lax.ppermute(pieces[step], 'row', perm))  23.7 us
    ppermute x9, starting transfers between devices, along_z(): out.append(lax.ppermute(pieces[step], 'row', perm))  23.3 us
    ppermute x12, waiting for transfers between devices, over_col(): have[h].append(lax.ppermute(joined[h], 'col', perm))  14.2 us
    ppermute x12, starting transfers between devices, over_col(): have[h].append(lax.ppermute(joined[h], 'col', perm))  13.3 us
  transfers between devices with their start and end apart: 44, of which 19 were waited for; matrix products, arithmetic and copies ran while one was open for 1% of the time, Pallas kernels for 34%

profile of v1, /device:TPU:0, one launch (start us, length us, event | category | flops | bytes accessed | tf_op | source)
XLA Modules:
  0.0 353.0 jit_solution(11010684084747337114)
XLA Ops:
  20.3 7.9 %collective-permute-done.2.refs_3_ = bf16[64,1536]{1,0:T(8,128)(2,1)S(1)} collective-permute-done((bf16[64,1536]{1,0:T(8,128)(2,1)S(1)}, bf16[64,1536]{1,0:T(8,128)(2,1)S(1)}, u32[]{:S(2)}, u32[]{:S(2)}) %collective-permute-start.2) | collective-permute-done | bytes 196640 | tf_op jit(solution)/shard_map/ppermute | solution.py:248
  33.1 4.7 %collective-permute-start.4 = (bf16[64,2304]{1,0:T(8,128)(2,1)S(1)}, bf16[64,2304]{1,0:T(8,128)(2,1)S(1)}, u32[]{:S(2)}, u32[]{:S(2)}) collective-permute-start(bf16[64,2304]{1,0:T(8,128)(2,1)S(1)} %get-tuple-element.126), channel_id=1, source_target_pairs={{0,8},{4,12},{8,16},{12,20},{16,24},{20,28},{24,0},{28,4},{1,9},{5... | collective-permute-start | bytes 884744 | tf_op jit(solution)/shard_map/ppermute | solution.py:248
  46.9 10.6 %collective-permute-done.5.refs_3_ = bf16[64,2304]{1,0:T(8,128)(2,1)S(1)} collective-permute-done((bf16[64,2304]{1,0:T(8,128)(2,1)S(1)}, bf16[64,2304]{1,0:T(8,128)(2,1)S(1)}, u32[]{:S(2)}, u32[]{:S(2)}) %collective-permute-start.5) | collective-permute-done | bytes 294944 | tf_op jit(solution)/shard_map/ppermute | solution.py:248
  62.9 3.7 %shard_map.105 = (bf16[512,1536]{1,0:T(8,128)(2,1)S(1)}, f8e4m3fn[512,1536]{1,0:T(32,128)(4,1)S(1)}, f32[8,128]{1,0:T(8,128)S(1)}, f32[8,128]{1,0:T(8,128)S(1)}) custom-call(bf16[512,1024]{1,0:T(8,128)(2,1)S(1)} %fusion.refs_0_, bf16[128,1536]{1,0:T(8,128)(2,1)S(1)} %get-tuple-element.129.refs_0_.refs_1_, ...), custom_call_target="tpu_custom_call" | custom-call | flops 1 | bytes 1 | tf_op jit(solution)/shard_map/pallas_call | solution.py:48
  68.6 6.8 %collective-permute-done.14.refs_1_.refs_2_ = bf16[128,2304]{1,0:T(8,128)(2,1)S(1)} collective-permute-done((bf16[128,2304]{1,0:T(8,128)(2,1)S(1)}, bf16[128,2304]{1,0:T(8,128)(2,1)S(1)}, u32[]{:S(2)}, u32[]{:S(2)}) %collective-permute-start.14) | collective-permute-done | bytes 589856 | tf_op jit(solution)/shard_map/ppermute | solution.py:273
  79.2 5.9 %collective-permute-start.10 = (bf16[64,2560]{1,0:T(8,128)(2,1)}, bf16[64,2560]{1,0:T(8,128)(2,1)S(1)}, u32[]{:S(2)}, u32[]{:S(2)}) collective-permute-start(bf16[64,2560]{1,0:T(8,128)(2,1)} %get-tuple-element.135), channel_id=1, source_target_pairs={{0,16},{4,20},{8,24},{12,28},{16,0},{20,4},{24,8},{28,12},{1,17},{... | collective-permute-start | bytes 983048 | tf_op jit(solution)/shard_map/ppermute | solution.py:248
  88.4 21.8 %shard_map.107 = (f32[512,6400]{1,0:T(8,128)}, f32[8,128]{1,0:T(8,128)}) custom-call(bf16[512,1536]{1,0:T(8,128)(2,1)} %copy-done.16, f8e4m3fn[512,1536]{1,0:T(32,128)(4,1)} %copy-done.20, f32[8,128]{1,0:T(8,128)} %copy-done.28, bf16[6400,6400]{1,0:T(8,128)(2,1)} %refs_3_.11, f32[8,128]{1,0:T(8,128)} %copy-done.30), custom_call_target="tpu_custom_call" | custom-call | flops 1 | bytes 1 | tf_op jit(solution)/shard_map/pallas_call | solution.py:48
  113.7 5.5 %shard_map.109 = (bf16[512,2304]{1,0:T(8,128)(2,1)S(1)}, f8e4m3fn[512,2304]{1,0:T(32,128)(4,1)S(1)}, f32[8,128]{1,0:T(8,128)S(1)}, f32[8,128]{1,0:T(8,128)S(1)}) custom-call(bf16[512,1024]{1,0:T(8,128)(2,1)S(1)} %fusion.refs_0_, bf16[128,2304]{1,0:T(8,128)(2,1)S(1)} %get-tuple-element.143.refs_0_.refs_1_, ...), custom_call_target="tpu_custom_call" | custom-call | flops 1 | bytes 1 | tf_op jit(solution)/shard_map/pallas_call | solution.py:48
  120.5 5.5 %collective-permute-done.16.refs_1_.refs_2_ = bf16[128,2560]{1,0:T(8,128)(2,1)S(1)} collective-permute-done((bf16[128,2560]{1,0:T(8,128)(2,1)S(1)}, bf16[128,2560]{1,0:T(8,128)(2,1)S(1)}, u32[]{:S(2)}, u32[]{:S(2)}) %collective-permute-start.16) | collective-permute-done | bytes 655392 | tf_op jit(solution)/shard_map/ppermute | solution.py:273
  131.1 32.0 %shard_map.111 = (f32[512,6400]{1,0:T(8,128)}, f32[8,128]{1,0:T(8,128)}) custom-call(bf16[512,2304]{1,0:T(8,128)(2,1)} %copy-done.13, f8e4m3fn[512,2304]{1,0:T(32,128)(4,1)} %copy-done.19, f32[8,128]{1,0:T(8,128)} %copy-done.29, bf16[6400,6400]{1,0:T(8,128)(2,1)} %refs_3_.11, ...), custom_call_target="tpu_custom_call", output_to_operand_aliasing={{0}: (4, {})} | custom-call | flops 1 | bytes 1 | tf_op jit(solution)/shard_map/pallas_call | solution.py:48
  163.8 6.0 %shard_map.112 = (bf16[512,2560]{1,0:T(8,128)(2,1)S(1)}, f8e4m3fn[512,2560]{1,0:T(32,128)(4,1)S(1)}, f32[8,128]{1,0:T(8,128)S(1)}, f32[8,128]{1,0:T(8,128)S(1)}) custom-call(bf16[512,1024]{1,0:T(8,128)(2,1)S(1)} %fusion.refs_0_, bf16[128,2560]{1,0:T(8,128)(2,1)S(1)} %get-tuple-element.148.refs_0_.refs_1_, ...), custom_call_target="tpu_custom_call" | custom-call | flops 1 | bytes 1 | tf_op jit(solution)/shard_map/pallas_call | solution.py:48
  173.5 17.7 %shard_map.113 = (f32[256,2560]{1,0:T(8,128)}, f32[256,2560]{1,0:T(8,128)}, f32[8,128]{1,0:T(8,128)}) custom-call(bf16[512,2560]{1,0:T(8,128)(2,1)} %copy-done.8, f8e4m3fn[512,2560]{1,0:T(32,128)(4,1)} %copy-done.10, f32[8,128]{1,0:T(8,128)} %copy-done.27, bf16[6400,6400]{1,0:T(8,128)(2,1)} %refs_3_.11, f32[512,6400]{1,0:T(8,128)} %get-tuple-element.165.refs_4_, ...), custom_call_target="tpu_custom_call" | custom-call | flops 1 | bytes 1 | tf_op jit(solution)/shard_map/pallas_call | solution.py:48
  193.8 4.9 %collective-permute-done.22.refs_1_ = f32[256,2560]{1,0:T(8,128)S(1)} collective-permute-done((f32[256,2560]{1,0:T(8,128)S(1)}, f32[256,2560]{1,0:T(8,128)S(1)}, u32[]{:S(2)}, u32[]{:S(2)}) %collective-permute-start.22) | collective-permute-done | bytes 2621472 | tf_op jit(solution)/shard_map/ppermute | solution.py:418
  201.8 7.0 %collective-permute-start.23 = (s16[272,1280]{1,0:T(8,128)(2,1)}, s16[272,1280]{1,0:T(8,128)(2,1)S(1)}, u32[]{:S(2)}, u32[]{:S(2)}) collective-permute-start(s16[272,1280]{1,0:T(8,128)(2,1)} %get-tuple-element.173), channel_id=1, source_target_pairs={{0,8},{4,12},{24,16},{28,20},{1,9},{5,13},{25,17},{29,21},{2,10},{... | collective-permute-start | bytes 2088968 | tf_op jit(solution)/shard_map/ppermute | solution.py:434
  208.8 23.4 %shard_map.116 = (f32[256,3840]{1,0:T(8,128)}, f32[256,3840]{1,0:T(8,128)}, f32[8,128]{1,0:T(8,128)}) custom-call(bf16[512,2560]{1,0:T(8,128)(2,1)} %copy-done.8, f8e4m3fn[512,2560]{1,0:T(32,128)(4,1)} %copy-done.10, f32[8,128]{1,0:T(8,128)} %copy-done.27, bf16[6400,6400]{1,0:T(8,128)(2,1)} %refs_3_.11, f32[512,6400]{1,0:T(8,128)} %get-tuple-element.165.refs_4_, ...), custom_call_target="tpu_custom_call" | custom-call | flops 1 | bytes 1 | tf_op jit(solution)/shard_map/pallas_call | solution.py:48
  268.8 7.4 %collective-permute-start.32 = (s16[272,1280]{1,0:T(8,128)(2,1)S(1)}, s16[272,1280]{1,0:T(8,128)(2,1)S(1)}, u32[]{:S(2)}, u32[]{:S(2)}) collective-permute-start(s16[272,1280]{1,0:T(8,128)(2,1)S(1)} %get-tuple-element.202), channel_id=1, source_target_pairs={{0,8},{4,12},{24,16},{28,20},{1,9},{5,13},{25,17},{29,21},{2,10},{... | collective-permute-start | bytes 2088968 | tf_op jit(solution)/shard_map/ppermute | solution.py:434
  276.2 3.5 shard_map.125
  283.8 9.0 %collective-permute-start.36 = (s16[272,1280]{1,0:T(8,128)(2,1)S(1)}, s16[272,1280]{1,0:T(8,128)(2,1)S(1)}, u32[]{:S(2)}, u32[]{:S(2)}) collective-permute-start(s16[272,1280]{1,0:T(8,128)(2,1)S(1)} %get-tuple-element.212), channel_id=1, source_target_pairs={{0,8},{4,12},{24,16},{28,20},{1,9},{5,13},{25,17},{29,21},{2,10},{... | collective-permute-start | bytes 2088968 | tf_op jit(solution)/shard_map/ppermute | solution.py:434
  297.9 10.4 %collective-permute-done.36.refs_1_ = s16[272,1280]{1,0:T(8,128)(2,1)S(1)} collective-permute-done((s16[272,1280]{1,0:T(8,128)(2,1)S(1)}, s16[272,1280]{1,0:T(8,128)(2,1)S(1)}, u32[]{:S(2)}, u32[]{:S(2)}) %collective-permute-start.36) | collective-permute-done | bytes 696352 | tf_op jit(solution)/shard_map/ppermute | solution.py:434
  318.5 3.5 %shard_map.134 = (bf16[128,1280]{1,0:T(8,128)(2,1)S(1)}, bf16[128,1280]{1,0:T(8,128)(2,1)S(1)}, f32[8,128]{1,0:T(8,128)S(1)}) custom-call(bf16[256,512]{1,0:T(8,128)(2,1)S(1)} %fusion.1.refs_0_, bf16[256,1280]{1,0:T(8,128)(2,1)S(1)} %get-tuple-element.220.refs_1_, bf16[256,1280]{1,0:T(8,128)(2,1)} %collective-permute-done.39.refs_2_, ...), custom_call_target="tpu_custom_call" | custom-call | flops 1 | bytes 1 | tf_op jit(solution)/shard_map/pallas_call | solution.py:48
  323.2 7.6 %collective-permute-done.33 = bf16[128,1280]{1,0:T(8,128)(2,1)S(1)} collective-permute-done((bf16[128,1280]{1,0:T(8,128)(2,1)}, bf16[128,1280]{1,0:T(8,128)(2,1)S(1)}, u32[]{:S(2)}, u32[]{:S(2)}) %collective-permute-start.33) | collective-permute-done | bytes 327712 | tf_op jit(solution)/shard_map/ppermute | solution.py:454
  332.2 5.4 %collective-permute-done.37 = bf16[128,1280]{1,0:T(8,128)(2,1)S(1)} collective-permute-done((bf16[128,1280]{1,0:T(8,128)(2,1)}, bf16[128,1280]{1,0:T(8,128)(2,1)S(1)}, u32[]{:S(2)}, u32[]{:S(2)}) %collective-permute-start.37) | collective-permute-done | bytes 327712 | tf_op jit(solution)/shard_map/ppermute | solution.py:454
  340.9 4.5 %collective-permute-done.40 = bf16[128,1280]{1,0:T(8,128)(2,1)S(1)} collective-permute-done((bf16[128,1280]{1,0:T(8,128)(2,1)S(1)}, bf16[128,1280]{1,0:T(8,128)(2,1)S(1)}, u32[]{:S(2)}, u32[]{:S(2)}) %collective-permute-start.40) | collective-permute-done | bytes 327712 | tf_op jit(solution)/shard_map/ppermute | solution.py:454
  345.5 6.7 %collective-permute-done.43 = bf16[128,1280]{1,0:T(8,128)(2,1)S(1)} collective-permute-done((bf16[128,1280]{1,0:T(8,128)(2,1)S(1)}, bf16[128,1280]{1,0:T(8,128)(2,1)S(1)}, u32[]{:S(2)}, u32[]{:S(2)}) %collective-permute-start.43) | collective-permute-done | bytes 327712 | tf_op jit(solution)/shard_map/ppermute | solution.py:454
  (219 shorter events, 130.4 us)
Async XLA Ops:
  12.4 15.8 %collective-permute-start.2 = (bf16[64,1536]{1,0:T(8,128)(2,1)S(1)}, bf16[64,1536]{1,0:T(8,128)(2,1)S(1)}, u32[]{:S(2)}, u32[]{:S(2)}) collective-permute-start(bf16[64,1536]{1,0:T(8,128)(2,1)S(1)} %get-tuple-element.123), channel_id=1, source_target_pairs={{0,16},{4,20},{8,24},{12,28},{16,0},{20,4},{24,8},{28,12},{1,17},{... | collective-permute-start | bytes 589832 | tf_op jit(solution)/shard_map/ppermute | solution.py:248
  37.8 19.7 %collective-permute-start.5 = (bf16[64,2304]{1,0:T(8,128)(2,1)S(1)}, bf16[64,2304]{1,0:T(8,128)(2,1)S(1)}, u32[]{:S(2)}, u32[]{:S(2)}) collective-permute-start(bf16[64,2304]{1,0:T(8,128)(2,1)S(1)} %get-tuple-element.127), channel_id=1, source_target_pairs={{0,16},{4,20},{8,24},{12,28},{16,0},{20,4},{24,8},{28,12},{1,17},{... | collective-permute-start | bytes 884744 | tf_op jit(solution)/shard_map/ppermute | solution.py:248
  39.4 18.1 %collective-permute-start.6 = (bf16[64,2304]{1,0:T(8,128)(2,1)S(1)}, bf16[64,2304]{1,0:T(8,128)(2,1)S(1)}, u32[]{:S(2)}, u32[]{:S(2)}) collective-permute-start(bf16[64,2304]{1,0:T(8,128)(2,1)S(1)} %get-tuple-element.128), channel_id=1, source_target_pairs={{0,24},{4,28},{8,0},{12,4},{16,8},{20,12},{24,16},{28,20},{1,25},{... | collective-permute-start | bytes 884744 | tf_op jit(solution)/shard_map/ppermute | solution.py:248
  42.3 20.5 %collective-permute-start.12 = (bf16[256,1536]{1,0:T(8,128)(2,1)S(1)}, bf16[256,1536]{1,0:T(8,128)(2,1)S(1)}, u32[]{:S(2)}, u32[]{:S(2)}) collective-permute-start(bf16[256,1536]{1,0:T(8,128)(2,1)S(1)} %get-tuple-element.137), channel_id=1, source_target_pairs={{0,2},{1,3},{2,0},{3,1},{4,6},{5,7},{6,4},{7,5},{8,10},{9,11},{10,... | collective-permute-start | bytes 2359304 | tf_op jit(solution)/shard_map/ppermute | solution.py:273
  43.9 18.9 %collective-permute-start.13 = (bf16[256,1536]{1,0:T(8,128)(2,1)S(1)}, bf16[256,1536]{1,0:T(8,128)(2,1)S(1)}, u32[]{:S(2)}, u32[]{:S(2)}) collective-permute-start(bf16[256,1536]{1,0:T(8,128)(2,1)S(1)} %get-tuple-element.138), channel_id=1, source_target_pairs={{0,1},{1,0},{2,3},{3,2},{4,5},{5,4},{6,7},{7,6},{8,9},{9,8},{10,11... | collective-permute-start | bytes 2359304 | tf_op jit(solution)/shard_map/ppermute | solution.py:273
  77.2 36.5 %collective-permute-start.18 = (bf16[256,2304]{1,0:T(8,128)(2,1)}, bf16[256,2304]{1,0:T(8,128)(2,1)S(1)}, u32[]{:S(2)}, u32[]{:S(2)}) collective-permute-start(bf16[256,2304]{1,0:T(8,128)(2,1)} %get-tuple-element.150), channel_id=1, source_target_pairs={{0,2},{1,3},{2,0},{3,1},{4,6},{5,7},{6,4},{7,5},{8,10},{9,11},{10,... | collective-permute-start | bytes 3538952 | tf_op jit(solution)/shard_map/ppermute | solution.py:273
  77.7 36.0 %collective-permute-start.19 = (bf16[256,2304]{1,0:T(8,128)(2,1)}, bf16[256,2304]{1,0:T(8,128)(2,1)S(1)}, u32[]{:S(2)}, u32[]{:S(2)}) collective-permute-start(bf16[256,2304]{1,0:T(8,128)(2,1)} %get-tuple-element.151), channel_id=1, source_target_pairs={{0,1},{1,0},{2,3},{3,2},{4,5},{5,4},{6,7},{7,6},{8,9},{9,8},{10,11... | collective-permute-start | bytes 3538952 | tf_op jit(solution)/shard_map/ppermute | solution.py:273
  79.2 31.0 %collective-permute-start.10 = (bf16[64,2560]{1,0:T(8,128)(2,1)}, bf16[64,2560]{1,0:T(8,128)(2,1)S(1)}, u32[]{:S(2)}, u32[]{:S(2)}) collective-permute-start(bf16[64,2560]{1,0:T(8,128)(2,1)} %get-tuple-element.135), channel_id=1, source_target_pairs={{0,16},{4,20},{8,24},{12,28},{16,0},{20,4},{24,8},{28,12},{1,17},{... | collective-permute-start | bytes 983048 | tf_op jit(solution)/shard_map/ppermute | solution.py:248
  85.0 25.2 %collective-permute-start.11 = (bf16[64,2560]{1,0:T(8,128)(2,1)}, bf16[64,2560]{1,0:T(8,128)(2,1)S(1)}, u32[]{:S(2)}, u32[]{:S(2)}) collective-permute-start(bf16[64,2560]{1,0:T(8,128)(2,1)} %get-tuple-element.136), channel_id=1, source_target_pairs={{0,24},{4,28},{8,0},{12,4},{16,8},{20,12},{24,16},{28,20},{1,25},{... | collective-permute-start | bytes 983048 | tf_op jit(solution)/shard_map/ppermute | solution.py:248
  88.4 21.8 %collective-permute-start.9 = (bf16[64,2560]{1,0:T(8,128)(2,1)}, bf16[64,2560]{1,0:T(8,128)(2,1)S(1)}, u32[]{:S(2)}, u32[]{:S(2)}) collective-permute-start(bf16[64,2560]{1,0:T(8,128)(2,1)} %get-tuple-element.134), channel_id=1, source_target_pairs={{0,8},{4,12},{8,16},{12,20},{16,24},{20,28},{24,0},{28,4},{1,9},{5... | collective-permute-start | bytes 983048 | tf_op jit(solution)/shard_map/ppermute | solution.py:248
  128.1 34.9 %collective-permute-start.20 = (bf16[256,2560]{1,0:T(8,128)(2,1)}, bf16[256,2560]{1,0:T(8,128)(2,1)S(1)}, u32[]{:S(2)}, u32[]{:S(2)}) collective-permute-start(bf16[256,2560]{1,0:T(8,128)(2,1)} %get-tuple-element.154), channel_id=1, source_target_pairs={{0,2},{1,3},{2,0},{3,1},{4,6},{5,7},{6,4},{7,5},{8,10},{9,11},{10,... | collective-permute-start | bytes 3932168 | tf_op jit(solution)/shard_map/ppermute | solution.py:273
  129.7 33.4 %collective-permute-start.21 = (bf16[256,2560]{1,0:T(8,128)(2,1)S(1)}, bf16[256,2560]{1,0:T(8,128)(2,1)S(1)}, u32[]{:S(2)}, u32[]{:S(2)}) collective-permute-start(bf16[256,2560]{1,0:T(8,128)(2,1)S(1)} %get-tuple-element.155), channel_id=1, source_target_pairs={{0,1},{1,0},{2,3},{3,2},{4,5},{5,4},{6,7},{7,6},{8,9},{9,8},{10,11... | collective-permute-start | bytes 3932168 | tf_op jit(solution)/shard_map/ppermute | solution.py:273
  201.8 30.4 %collective-permute-start.23 = (s16[272,1280]{1,0:T(8,128)(2,1)}, s16[272,1280]{1,0:T(8,128)(2,1)S(1)}, u32[]{:S(2)}, u32[]{:S(2)}) collective-permute-start(s16[272,1280]{1,0:T(8,128)(2,1)} %get-tuple-element.173), channel_id=1, source_target_pairs={{0,8},{4,12},{24,16},{28,20},{1,9},{5,13},{25,17},{29,21},{2,10},{... | collective-permute-start | bytes 2088968 | tf_op jit(solution)/shard_map/ppermute | solution.py:434
  240.8 17.7 %collective-permute-start.26 = (s16[272,1280]{1,0:T(8,128)(2,1)}, s16[272,1280]{1,0:T(8,128)(2,1)}, u32[]{:S(2)}, u32[]{:S(2)}) collective-permute-start(s16[272,1280]{1,0:T(8,128)(2,1)} %get-tuple-element.184), channel_id=1, source_target_pairs={{0,8},{4,12},{24,16},{28,20},{1,9},{5,13},{25,17},{29,21},{2,10},{... | collective-permute-start | bytes 2088968 | tf_op jit(solution)/shard_map/ppermute | solution.py:434
  243.2 21.5 %collective-permute-start.24 = (s16[272,1280]{1,0:T(8,128)(2,1)}, s16[272,1280]{1,0:T(8,128)(2,1)}, u32[]{:S(2)}, u32[]{:S(2)}) collective-permute-start(s16[272,1280]{1,0:T(8,128)(2,1)} %get-tuple-element.177), channel_id=1, source_target_pairs={{8,16},{12,20},{16,8},{20,12},{9,17},{13,21},{17,9},{21,13},{10,18... | collective-permute-start | bytes 2088968 | tf_op jit(solution)/shard_map/ppermute | solution.py:434
  250.5 25.7 %collective-permute-start.28 = (s16[272,1280]{1,0:T(8,128)(2,1)}, s16[272,1280]{1,0:T(8,128)(2,1)}, u32[]{:S(2)}, u32[]{:S(2)}) collective-permute-start(s16[272,1280]{1,0:T(8,128)(2,1)} %get-tuple-element.192), channel_id=1, source_target_pairs={{0,8},{4,12},{24,16},{28,20},{1,9},{5,13},{25,17},{29,21},{2,10},{... | collective-permute-start | bytes 2088968 | tf_op jit(solution)/shard_map/ppermute | solution.py:434
  267.7 15.5 %collective-permute-start.30 = (s16[272,1280]{1,0:T(8,128)(2,1)S(1)}, s16[272,1280]{1,0:T(8,128)(2,1)S(1)}, u32[]{:S(2)}, u32[]{:S(2)}) collective-permute-start(s16[272,1280]{1,0:T(8,128)(2,1)S(1)} %get-tuple-element.198), channel_id=1, source_target_pairs={{8,16},{12,20},{16,8},{20,12},{9,17},{13,21},{17,9},{21,13},{10,18... | collective-permute-start | bytes 2088968 | tf_op jit(solution)/shard_map/ppermute | solution.py:434
  268.8 24.0 %collective-permute-start.32 = (s16[272,1280]{1,0:T(8,128)(2,1)S(1)}, s16[272,1280]{1,0:T(8,128)(2,1)S(1)}, u32[]{:S(2)}, u32[]{:S(2)}) collective-permute-start(s16[272,1280]{1,0:T(8,128)(2,1)S(1)} %get-tuple-element.202), channel_id=1, source_target_pairs={{0,8},{4,12},{24,16},{28,20},{1,9},{5,13},{25,17},{29,21},{2,10},{... | collective-permute-start | bytes 2088968 | tf_op jit(solution)/shard_map/ppermute | solution.py:434
  279.6 16.2 %collective-permute-start.34 = (s16[272,1280]{1,0:T(8,128)(2,1)S(1)}, s16[272,1280]{1,0:T(8,128)(2,1)S(1)}, u32[]{:S(2)}, u32[]{:S(2)}) collective-permute-start(s16[272,1280]{1,0:T(8,128)(2,1)S(1)} %get-tuple-element.208), channel_id=1, source_target_pairs={{8,16},{12,20},{16,8},{20,12},{9,17},{13,21},{17,9},{21,13},{10,18... | collective-permute-start | bytes 2088968 | tf_op jit(solution)/shard_map/ppermute | solution.py:434
  283.8 24.5 %collective-permute-start.36 = (s16[272,1280]{1,0:T(8,128)(2,1)S(1)}, s16[272,1280]{1,0:T(8,128)(2,1)S(1)}, u32[]{:S(2)}, u32[]{:S(2)}) collective-permute-start(s16[272,1280]{1,0:T(8,128)(2,1)S(1)} %get-tuple-element.212), channel_id=1, source_target_pairs={{0,8},{4,12},{24,16},{28,20},{1,9},{5,13},{25,17},{29,21},{2,10},{... | collective-permute-start | bytes 2088968 | tf_op jit(solution)/shard_map/ppermute | solution.py:434
  293.7 19.8 %collective-permute-start.38 = (s16[272,1280]{1,0:T(8,128)(2,1)S(1)}, s16[272,1280]{1,0:T(8,128)(2,1)S(1)}, u32[]{:S(2)}, u32[]{:S(2)}) collective-permute-start(s16[272,1280]{1,0:T(8,128)(2,1)S(1)} %get-tuple-element.218), channel_id=1, source_target_pairs={{8,16},{12,20},{16,8},{20,12},{9,17},{13,21},{17,9},{21,13},{10,18... | collective-permute-start | bytes 2088968 | tf_op jit(solution)/shard_map/ppermute | solution.py:434
  296.6 19.5 %collective-permute-start.29 = (bf16[128,1280]{1,0:T(8,128)(2,1)}, bf16[128,1280]{1,0:T(8,128)(2,1)}, u32[]{:S(2)}, u32[]{:S(2)}) collective-permute-start(bf16[128,1280]{1,0:T(8,128)(2,1)} %get-tuple-element.195), channel_id=1, source_target_pairs={{8,0},{12,4},{16,24},{20,28},{9,1},{13,5},{17,25},{21,29},{10,2},{... | collective-permute-start | bytes 983048 | tf_op jit(solution)/shard_map/ppermute | solution.py:454
  314.8 15.9 %collective-permute-start.33 = (bf16[128,1280]{1,0:T(8,128)(2,1)}, bf16[128,1280]{1,0:T(8,128)(2,1)S(1)}, u32[]{:S(2)}, u32[]{:S(2)}) collective-permute-start(bf16[128,1280]{1,0:T(8,128)(2,1)} %copy-done.38), channel_id=1, source_target_pairs={{8,0},{12,4},{16,24},{20,28},{9,1},{13,5},{17,25},{21,29},{10,2},{... | collective-permute-start | bytes 983048 | tf_op jit(solution)/shard_map/ppermute | solution.py:454
  317.2 20.4 %collective-permute-start.37 = (bf16[128,1280]{1,0:T(8,128)(2,1)}, bf16[128,1280]{1,0:T(8,128)(2,1)S(1)}, u32[]{:S(2)}, u32[]{:S(2)}) collective-permute-start(bf16[128,1280]{1,0:T(8,128)(2,1)} %copy-done.39), channel_id=1, source_target_pairs={{8,0},{12,4},{16,24},{20,28},{9,1},{13,5},{17,25},{21,29},{10,2},{... | collective-permute-start | bytes 983048 | tf_op jit(solution)/shard_map/ppermute | solution.py:454
  (68 other events, 458.6 us)

commit v2 on v1

--- a/solution.py
+++ b/solution.py
@@ -18,7 +18,7 @@
 MIB = 1024 * 1024
 COST = 1
 ORDER = (
-    (0, 0), (1, 0), (2, 0), (0, 1), (3, 0), (2, 1), (1, 1), (2, 2), (2, 3), (3, 1), (2, 4), (4, 0), (3, 2), (5, 0), (4, 1),
+    (0, 0), (1, 0), (2, 0), (2, 1), (0, 1), (3, 0), (3, 1), (1, 1), (2, 2), (2, 3), (2, 4), (4, 0), (4, 1), (3, 2), (5, 0),
     (3, 3), (5, 1), (4, 2), (3, 4), (5, 2), (4, 3), (5, 3), (4, 4), (5, 4),
 )
 
@@ -412,9 +412,10 @@
         own, foreign = groups[group]
         anywhere = pl.BlockSpec(memory_space=pl.ANY)
         shape = jax.ShapeDtypeStruct(foreign.shape, foreign.dtype)
-        (foreign,) = chain.call(
-            lambda *refs: None, [foreign], [anywhere], [anywhere], [shape], (1,), input_output_aliases={0: 0}
-        )
+        if group:
+            (foreign,) = chain.call(
+                lambda *refs: None, [foreign], [anywhere], [anywhere], [shape], (1,), input_output_aliases={0: 0}
+            )
         groups[group] = [own, lax.ppermute(foreign, "row", siblings)]
 
     def begin(part):

time: 354 us -> 350 us (0.989)
  local copies, waits for them, and re-layouts: 26.1 us -> 20.5 us
    unnamed x96 -> x88, local copies, waits for them, and re-layouts: 25.6 us -> 20 us
    ppermute x10, starting transfers between devices: 32.3 us -> 36.3 us  [inward(): return (value, lax.ppermute(code, 'row', perm))]
    ppermute x10, waiting for transfers between devices: 11.2 us -> 7.28 us  [inward(): return (value, lax.ppermute(code, 'row', perm))]
    ppermute x5, waiting for transfers between devices: 24.2 us -> 28 us  [spread(): rest = lax.ppermute(rest, 'row', perm)]
    pallas_call x37 -> x36, Pallas kernels: 159 us -> 157 us  [call(): pl.pallas_call(wrapped, grid_spec=pltpu.PrefetchScalarGridSpec(num_scalar...]
  transfers between devices with their start and end apart: 44 -> 44, of which waited for: 19 -> 20; matrix products, arithmetic and copies ran while one was open for 1% -> 1% of each run, Pallas kernels for 34% -> 35%
where the time goes in v2:
time: 350 us; the launch traced here: 349 us
  Pallas kernels  157 us (45%)
  waiting for transfers between devices  85.2 us (24%)
  starting transfers between devices  80.2 us (23%)
  local copies, waits for them, and re-layouts  20.5 us (6%)
  other arithmetic  5.01 us (1%)
    pallas_call x36, Pallas kernels, call(): pl.pallas_call(wrapped, grid_spec=pltpu.PrefetchScalarGridSpec(num_scalar...  157 us
    ppermute x10, starting transfers between devices, inward(): return (value, lax.ppermute(code, 'row', perm))  36.3 us
    ppermute x5, waiting for transfers between devices, spread(): rest = lax.ppermute(rest, 'row', perm)  28 us
    ppermute x9, waiting for transfers between devices, along_z(): out.append(lax.ppermute(pieces[step], 'row', perm))  23.7 us
    ppermute x9, starting transfers between devices, along_z(): out.append(lax.ppermute(pieces[step], 'row', perm))  23.3 us
    unnamed x88, local copies, waits for them, and re-layouts  20 us
    ppermute x12, waiting for transfers between devices, over_col(): have[h].append(lax.ppermute(joined[h], 'col', perm))  14.1 us
    ppermute x12, starting transfers between devices, over_col(): have[h].append(lax.ppermute(joined[h], 'col', perm))  13.3 us
  transfers between devices with their start and end apart: 44, of which 20 were waited for; matrix products, arithmetic and copies ran while one was open for 1% of the time, Pallas kernels for 35%

profile of v2, /device:TPU:0, one launch (start us, length us, event | category | flops | bytes accessed | tf_op | source)
XLA Modules:
  0.0 348.9 jit_solution(3321407874621384216)
XLA Ops:
  20.3 7.9 %collective-permute-done.2.refs_3_ = bf16[64,1536]{1,0:T(8,128)(2,1)S(1)} collective-permute-done((bf16[64,1536]{1,0:T(8,128)(2,1)S(1)}, bf16[64,1536]{1,0:T(8,128)(2,1)S(1)}, u32[]{:S(2)}, u32[]{:S(2)}) %collective-permute-start.2) | collective-permute-done | bytes 196640 | tf_op jit(solution)/shard_map/ppermute | solution.py:248
  33.1 4.7 %collective-permute-start.4 = (bf16[64,2304]{1,0:T(8,128)(2,1)S(1)}, bf16[64,2304]{1,0:T(8,128)(2,1)S(1)}, u32[]{:S(2)}, u32[]{:S(2)}) collective-permute-start(bf16[64,2304]{1,0:T(8,128)(2,1)S(1)} %get-tuple-element.124), channel_id=1, source_target_pairs={{0,8},{4,12},{8,16},{12,20},{16,24},{20,28},{24,0},{28,4},{1,9},{5... | collective-permute-start | bytes 884744 | tf_op jit(solution)/shard_map/ppermute | solution.py:248
  46.9 10.6 %collective-permute-done.5.refs_3_ = bf16[64,2304]{1,0:T(8,128)(2,1)S(1)} collective-permute-done((bf16[64,2304]{1,0:T(8,128)(2,1)S(1)}, bf16[64,2304]{1,0:T(8,128)(2,1)S(1)}, u32[]{:S(2)}, u32[]{:S(2)}) %collective-permute-start.5) | collective-permute-done | bytes 294944 | tf_op jit(solution)/shard_map/ppermute | solution.py:248
  62.9 3.7 %shard_map.105 = (bf16[512,1536]{1,0:T(8,128)(2,1)S(1)}, f8e4m3fn[512,1536]{1,0:T(32,128)(4,1)S(1)}, f32[8,128]{1,0:T(8,128)S(1)}, f32[8,128]{1,0:T(8,128)S(1)}) custom-call(bf16[512,1024]{1,0:T(8,128)(2,1)S(1)} %fusion.refs_0_, bf16[128,1536]{1,0:T(8,128)(2,1)S(1)} %get-tuple-element.127.refs_0_.refs_1_, ...), custom_call_target="tpu_custom_call" | custom-call | flops 1 | bytes 1 | tf_op jit(solution)/shard_map/pallas_call | solution.py:48
  68.6 6.8 %collective-permute-done.14.refs_1_.refs_2_ = bf16[128,2304]{1,0:T(8,128)(2,1)S(1)} collective-permute-done((bf16[128,2304]{1,0:T(8,128)(2,1)S(1)}, bf16[128,2304]{1,0:T(8,128)(2,1)S(1)}, u32[]{:S(2)}, u32[]{:S(2)}) %collective-permute-start.14) | collective-permute-done | bytes 589856 | tf_op jit(solution)/shard_map/ppermute | solution.py:273
  79.2 5.9 %collective-permute-start.10 = (bf16[64,2560]{1,0:T(8,128)(2,1)}, bf16[64,2560]{1,0:T(8,128)(2,1)S(1)}, u32[]{:S(2)}, u32[]{:S(2)}) collective-permute-start(bf16[64,2560]{1,0:T(8,128)(2,1)} %get-tuple-element.133), channel_id=1, source_target_pairs={{0,16},{4,20},{8,24},{12,28},{16,0},{20,4},{24,8},{28,12},{1,17},{... | collective-permute-start | bytes 983048 | tf_op jit(solution)/shard_map/ppermute | solution.py:248
  88.5 21.8 %shard_map.107 = (f32[512,6400]{1,0:T(8,128)}, f32[8,128]{1,0:T(8,128)}) custom-call(bf16[512,1536]{1,0:T(8,128)(2,1)} %copy-done.13, f8e4m3fn[512,1536]{1,0:T(32,128)(4,1)} %copy-done.17, f32[8,128]{1,0:T(8,128)} %copy-done.24, bf16[6400,6400]{1,0:T(8,128)(2,1)} %refs_3_.11, f32[8,128]{1,0:T(8,128)} %copy-done.26), custom_call_target="tpu_custom_call" | custom-call | flops 1 | bytes 1 | tf_op jit(solution)/shard_map/pallas_call | solution.py:48
  113.8 5.5 %shard_map.109 = (bf16[512,2304]{1,0:T(8,128)(2,1)S(1)}, f8e4m3fn[512,2304]{1,0:T(32,128)(4,1)S(1)}, f32[8,128]{1,0:T(8,128)S(1)}, f32[8,128]{1,0:T(8,128)S(1)}) custom-call(bf16[512,1024]{1,0:T(8,128)(2,1)S(1)} %fusion.refs_0_, bf16[128,2304]{1,0:T(8,128)(2,1)S(1)} %get-tuple-element.141.refs_0_.refs_1_, ...), custom_call_target="tpu_custom_call" | custom-call | flops 1 | bytes 1 | tf_op jit(solution)/shard_map/pallas_call | solution.py:48
  120.7 5.4 %collective-permute-done.16.refs_1_.refs_2_ = bf16[128,2560]{1,0:T(8,128)(2,1)S(1)} collective-permute-done((bf16[128,2560]{1,0:T(8,128)(2,1)S(1)}, bf16[128,2560]{1,0:T(8,128)(2,1)S(1)}, u32[]{:S(2)}, u32[]{:S(2)}) %collective-permute-start.16) | collective-permute-done | bytes 655392 | tf_op jit(solution)/shard_map/ppermute | solution.py:273
  131.1 32.0 %shard_map.111 = (f32[512,6400]{1,0:T(8,128)}, f32[8,128]{1,0:T(8,128)}) custom-call(bf16[512,2304]{1,0:T(8,128)(2,1)} %copy-done.10, f8e4m3fn[512,2304]{1,0:T(32,128)(4,1)} %copy-done.16, f32[8,128]{1,0:T(8,128)} %copy-done.25, bf16[6400,6400]{1,0:T(8,128)(2,1)} %refs_3_.11, ...), custom_call_target="tpu_custom_call", output_to_operand_aliasing={{0}: (4, {})} | custom-call | flops 1 | bytes 1 | tf_op jit(solution)/shard_map/pallas_call | solution.py:48
  163.8 6.0 %shard_map.112 = (bf16[512,2560]{1,0:T(8,128)(2,1)S(1)}, f8e4m3fn[512,2560]{1,0:T(32,128)(4,1)S(1)}, f32[8,128]{1,0:T(8,128)S(1)}, f32[8,128]{1,0:T(8,128)S(1)}) custom-call(bf16[512,1024]{1,0:T(8,128)(2,1)S(1)} %fusion.refs_0_, bf16[128,2560]{1,0:T(8,128)(2,1)S(1)} %get-tuple-element.146.refs_0_.refs_1_, ...), custom_call_target="tpu_custom_call" | custom-call | flops 1 | bytes 1 | tf_op jit(solution)/shard_map/pallas_call | solution.py:48
  173.0 18.0 %shard_map.113 = (f32[256,2560]{1,0:T(8,128)}, f32[256,2560]{1,0:T(8,128)}, f32[8,128]{1,0:T(8,128)}) custom-call(bf16[512,2560]{1,0:T(8,128)(2,1)} %copy-done.6, f8e4m3fn[512,2560]{1,0:T(32,128)(4,1)} %copy-done.8, f32[8,128]{1,0:T(8,128)} %copy-done.23, bf16[6400,6400]{1,0:T(8,128)(2,1)} %refs_3_.11, f32[512,6400]{1,0:T(8,128)} %get-tuple-element.163.refs_4_, ...), custom_call_target="tpu_custom_call" | custom-call | flops 1 | bytes 1 | tf_op jit(solution)/shard_map/pallas_call | solution.py:48
  191.0 5.1 %collective-permute-done.22.refs_1_ = f32[256,2560]{1,0:T(8,128)S(1)} collective-permute-done((f32[256,2560]{1,0:T(8,128)}, f32[256,2560]{1,0:T(8,128)S(1)}, u32[]{:S(2)}, u32[]{:S(2)}) %collective-permute-start.22) | collective-permute-done | bytes 2621472 | tf_op jit(solution)/shard_map/ppermute | solution.py:419
  199.4 6.9 %collective-permute-start.23 = (s16[272,1280]{1,0:T(8,128)(2,1)S(1)}, s16[272,1280]{1,0:T(8,128)(2,1)S(1)}, u32[]{:S(2)}, u32[]{:S(2)}) collective-permute-start(s16[272,1280]{1,0:T(8,128)(2,1)S(1)} %get-tuple-element.169), channel_id=1, source_target_pairs={{0,8},{4,12},{24,16},{28,20},{1,9},{5,13},{25,17},{29,21},{2,10},{... | collective-permute-start | bytes 2088968 | tf_op jit(solution)/shard_map/ppermute | solution.py:435
  209.1 23.5 %shard_map.116 = (f32[256,3840]{1,0:T(8,128)}, f32[256,3840]{1,0:T(8,128)}, f32[8,128]{1,0:T(8,128)}) custom-call(bf16[512,2560]{1,0:T(8,128)(2,1)} %copy-done.6, f8e4m3fn[512,2560]{1,0:T(32,128)(4,1)} %copy-done.8, f32[8,128]{1,0:T(8,128)} %copy-done.23, bf16[6400,6400]{1,0:T(8,128)(2,1)} %refs_3_.11, f32[512,6400]{1,0:T(8,128)} %get-tuple-element.163.refs_4_, ...), custom_call_target="tpu_custom_call" | custom-call | flops 1 | bytes 1 | tf_op jit(solution)/shard_map/pallas_call | solution.py:48
  242.0 3.6 %collective-permute-done.26.refs_1_ = f32[256,3840]{1,0:T(8,128)S(1)} collective-permute-done((f32[256,3840]{1,0:T(8,128)S(1)}, f32[256,3840]{1,0:T(8,128)S(1)}, u32[]{:S(2)}, u32[]{:S(2)}) %collective-permute-start.26) | collective-permute-done | bytes 3932192 | tf_op jit(solution)/shard_map/ppermute | solution.py:419
  249.6 4.4 %collective-permute-start.28 = (s16[272,1280]{1,0:T(8,128)(2,1)}, s16[272,1280]{1,0:T(8,128)(2,1)S(1)}, u32[]{:S(2)}, u32[]{:S(2)}) collective-permute-start(s16[272,1280]{1,0:T(8,128)(2,1)} %get-tuple-element.188), channel_id=1, source_target_pairs={{0,8},{4,12},{24,16},{28,20},{1,9},{5,13},{25,17},{29,21},{2,10},{... | collective-permute-start | bytes 2088968 | tf_op jit(solution)/shard_map/ppermute | solution.py:435
  263.2 4.4 %collective-permute-start.32 = (s16[272,1280]{1,0:T(8,128)(2,1)S(1)}, s16[272,1280]{1,0:T(8,128)(2,1)S(1)}, u32[]{:S(2)}, u32[]{:S(2)}) collective-permute-start(s16[272,1280]{1,0:T(8,128)(2,1)S(1)} %get-tuple-element.198), channel_id=1, source_target_pairs={{0,8},{4,12},{24,16},{28,20},{1,9},{5,13},{25,17},{29,21},{2,10},{... | collective-permute-start | bytes 2088968 | tf_op jit(solution)/shard_map/ppermute | solution.py:435
  273.1 13.9 %collective-permute-start.36 = (s16[272,1280]{1,0:T(8,128)(2,1)S(1)}, s16[272,1280]{1,0:T(8,128)(2,1)S(1)}, u32[]{:S(2)}, u32[]{:S(2)}) collective-permute-start(s16[272,1280]{1,0:T(8,128)(2,1)S(1)} %get-tuple-element.208), channel_id=1, source_target_pairs={{0,8},{4,12},{24,16},{28,20},{1,9},{5,13},{25,17},{29,21},{2,10},{... | collective-permute-start | bytes 2088968 | tf_op jit(solution)/shard_map/ppermute | solution.py:435
  295.5 6.7 %collective-permute-done.36.refs_1_ = s16[272,1280]{1,0:T(8,128)(2,1)S(1)} collective-permute-done((s16[272,1280]{1,0:T(8,128)(2,1)S(1)}, s16[272,1280]{1,0:T(8,128)(2,1)S(1)}, u32[]{:S(2)}, u32[]{:S(2)}) %collective-permute-start.36) | collective-permute-done | bytes 696352 | tf_op jit(solution)/shard_map/ppermute | solution.py:435
  318.4 8.6 %collective-permute-done.33 = bf16[128,1280]{1,0:T(8,128)(2,1)S(1)} collective-permute-done((bf16[128,1280]{1,0:T(8,128)(2,1)}, bf16[128,1280]{1,0:T(8,128)(2,1)S(1)}, u32[]{:S(2)}, u32[]{:S(2)}) %collective-permute-start.33) | collective-permute-done | bytes 327712 | tf_op jit(solution)/shard_map/ppermute | solution.py:455
  328.3 5.4 %collective-permute-done.37 = bf16[128,1280]{1,0:T(8,128)(2,1)S(1)} collective-permute-done((bf16[128,1280]{1,0:T(8,128)(2,1)}, bf16[128,1280]{1,0:T(8,128)(2,1)S(1)}, u32[]{:S(2)}, u32[]{:S(2)}) %collective-permute-start.37) | collective-permute-done | bytes 327712 | tf_op jit(solution)/shard_map/ppermute | solution.py:455
  337.1 4.2 %collective-permute-done.40 = bf16[128,1280]{1,0:T(8,128)(2,1)S(1)} collective-permute-done((bf16[128,1280]{1,0:T(8,128)(2,1)S(1)}, bf16[128,1280]{1,0:T(8,128)(2,1)S(1)}, u32[]{:S(2)}, u32[]{:S(2)}) %collective-permute-start.40) | collective-permute-done | bytes 327712 | tf_op jit(solution)/shard_map/ppermute | solution.py:455
  341.4 6.7 %collective-permute-done.43 = bf16[128,1280]{1,0:T(8,128)(2,1)S(1)} collective-permute-done((bf16[128,1280]{1,0:T(8,128)(2,1)S(1)}, bf16[128,1280]{1,0:T(8,128)(2,1)S(1)}, u32[]{:S(2)}, u32[]{:S(2)}) %collective-permute-start.43) | collective-permute-done | bytes 327712 | tf_op jit(solution)/shard_map/ppermute | solution.py:455
  (210 shorter events, 125.8 us)
Async XLA Ops:
  37.8 19.7 %collective-permute-start.5 = (bf16[64,2304]{1,0:T(8,128)(2,1)S(1)}, bf16[64,2304]{1,0:T(8,128)(2,1)S(1)}, u32[]{:S(2)}, u32[]{:S(2)}) collective-permute-start(bf16[64,2304]{1,0:T(8,128)(2,1)S(1)} %get-tuple-element.125), channel_id=1, source_target_pairs={{0,16},{4,20},{8,24},{12,28},{16,0},{20,4},{24,8},{28,12},{1,17},{... | collective-permute-start | bytes 884744 | tf_op jit(solution)/shard_map/ppermute | solution.py:248
  39.4 18.1 %collective-permute-start.6 = (bf16[64,2304]{1,0:T(8,128)(2,1)S(1)}, bf16[64,2304]{1,0:T(8,128)(2,1)S(1)}, u32[]{:S(2)}, u32[]{:S(2)}) collective-permute-start(bf16[64,2304]{1,0:T(8,128)(2,1)S(1)} %get-tuple-element.126), channel_id=1, source_target_pairs={{0,24},{4,28},{8,0},{12,4},{16,8},{20,12},{24,16},{28,20},{1,25},{... | collective-permute-start | bytes 884744 | tf_op jit(solution)/shard_map/ppermute | solution.py:248
  42.3 20.5 %collective-permute-start.12 = (bf16[256,1536]{1,0:T(8,128)(2,1)S(1)}, bf16[256,1536]{1,0:T(8,128)(2,1)S(1)}, u32[]{:S(2)}, u32[]{:S(2)}) collective-permute-start(bf16[256,1536]{1,0:T(8,128)(2,1)S(1)} %get-tuple-element.135), channel_id=1, source_target_pairs={{0,2},{1,3},{2,0},{3,1},{4,6},{5,7},{6,4},{7,5},{8,10},{9,11},{10,... | collective-permute-start | bytes 2359304 | tf_op jit(solution)/shard_map/ppermute | solution.py:273
  43.9 19.0 %collective-permute-start.13 = (bf16[256,1536]{1,0:T(8,128)(2,1)S(1)}, bf16[256,1536]{1,0:T(8,128)(2,1)S(1)}, u32[]{:S(2)}, u32[]{:S(2)}) collective-permute-start(bf16[256,1536]{1,0:T(8,128)(2,1)S(1)} %get-tuple-element.136), channel_id=1, source_target_pairs={{0,1},{1,0},{2,3},{3,2},{4,5},{5,4},{6,7},{7,6},{8,9},{9,8},{10,11... | collective-permute-start | bytes 2359304 | tf_op jit(solution)/shard_map/ppermute | solution.py:273
  77.2 36.6 %collective-permute-start.18 = (bf16[256,2304]{1,0:T(8,128)(2,1)}, bf16[256,2304]{1,0:T(8,128)(2,1)S(1)}, u32[]{:S(2)}, u32[]{:S(2)}) collective-permute-start(bf16[256,2304]{1,0:T(8,128)(2,1)} %get-tuple-element.148), channel_id=1, source_target_pairs={{0,2},{1,3},{2,0},{3,1},{4,6},{5,7},{6,4},{7,5},{8,10},{9,11},{10,... | collective-permute-start | bytes 3538952 | tf_op jit(solution)/shard_map/ppermute | solution.py:273
  77.7 36.1 %collective-permute-start.19 = (bf16[256,2304]{1,0:T(8,128)(2,1)}, bf16[256,2304]{1,0:T(8,128)(2,1)S(1)}, u32[]{:S(2)}, u32[]{:S(2)}) collective-permute-start(bf16[256,2304]{1,0:T(8,128)(2,1)} %get-tuple-element.149), channel_id=1, source_target_pairs={{0,1},{1,0},{2,3},{3,2},{4,5},{5,4},{6,7},{7,6},{8,9},{9,8},{10,11... | collective-permute-start | bytes 3538952 | tf_op jit(solution)/shard_map/ppermute | solution.py:273
  79.2 31.1 %collective-permute-start.10 = (bf16[64,2560]{1,0:T(8,128)(2,1)}, bf16[64,2560]{1,0:T(8,128)(2,1)S(1)}, u32[]{:S(2)}, u32[]{:S(2)}) collective-permute-start(bf16[64,2560]{1,0:T(8,128)(2,1)} %get-tuple-element.133), channel_id=1, source_target_pairs={{0,16},{4,20},{8,24},{12,28},{16,0},{20,4},{24,8},{28,12},{1,17},{... | collective-permute-start | bytes 983048 | tf_op jit(solution)/shard_map/ppermute | solution.py:248
  85.1 25.2 %collective-permute-start.11 = (bf16[64,2560]{1,0:T(8,128)(2,1)}, bf16[64,2560]{1,0:T(8,128)(2,1)S(1)}, u32[]{:S(2)}, u32[]{:S(2)}) collective-permute-start(bf16[64,2560]{1,0:T(8,128)(2,1)} %get-tuple-element.134), channel_id=1, source_target_pairs={{0,24},{4,28},{8,0},{12,4},{16,8},{20,12},{24,16},{28,20},{1,25},{... | collective-permute-start | bytes 983048 | tf_op jit(solution)/shard_map/ppermute | solution.py:248
  88.4 21.9 %collective-permute-start.9 = (bf16[64,2560]{1,0:T(8,128)(2,1)}, bf16[64,2560]{1,0:T(8,128)(2,1)S(1)}, u32[]{:S(2)}, u32[]{:S(2)}) collective-permute-start(bf16[64,2560]{1,0:T(8,128)(2,1)} %get-tuple-element.132), channel_id=1, source_target_pairs={{0,8},{4,12},{8,16},{12,20},{16,24},{20,28},{24,0},{28,4},{1,9},{5... | collective-permute-start | bytes 983048 | tf_op jit(solution)/shard_map/ppermute | solution.py:248
  128.1 35.0 %collective-permute-start.20 = (bf16[256,2560]{1,0:T(8,128)(2,1)}, bf16[256,2560]{1,0:T(8,128)(2,1)S(1)}, u32[]{:S(2)}, u32[]{:S(2)}) collective-permute-start(bf16[256,2560]{1,0:T(8,128)(2,1)} %get-tuple-element.152), channel_id=1, source_target_pairs={{0,2},{1,3},{2,0},{3,1},{4,6},{5,7},{6,4},{7,5},{8,10},{9,11},{10,... | collective-permute-start | bytes 3932168 | tf_op jit(solution)/shard_map/ppermute | solution.py:273
  129.7 33.5 %collective-permute-start.21 = (bf16[256,2560]{1,0:T(8,128)(2,1)}, bf16[256,2560]{1,0:T(8,128)(2,1)S(1)}, u32[]{:S(2)}, u32[]{:S(2)}) collective-permute-start(bf16[256,2560]{1,0:T(8,128)(2,1)} %get-tuple-element.153), channel_id=1, source_target_pairs={{0,1},{1,0},{2,3},{3,2},{4,5},{5,4},{6,7},{7,6},{8,9},{9,8},{10,11... | collective-permute-start | bytes 3932168 | tf_op jit(solution)/shard_map/ppermute | solution.py:273
  199.4 33.2 %collective-permute-start.23 = (s16[272,1280]{1,0:T(8,128)(2,1)S(1)}, s16[272,1280]{1,0:T(8,128)(2,1)S(1)}, u32[]{:S(2)}, u32[]{:S(2)}) collective-permute-start(s16[272,1280]{1,0:T(8,128)(2,1)S(1)} %get-tuple-element.169), channel_id=1, source_target_pairs={{0,8},{4,12},{24,16},{28,20},{1,9},{5,13},{25,17},{29,21},{2,10},{... | collective-permute-start | bytes 2088968 | tf_op jit(solution)/shard_map/ppermute | solution.py:435
  207.8 28.6 %collective-permute-start.25 = (s16[272,1280]{1,0:T(8,128)(2,1)S(1)}, s16[272,1280]{1,0:T(8,128)(2,1)S(1)}, u32[]{:S(2)}, u32[]{:S(2)}) collective-permute-start(s16[272,1280]{1,0:T(8,128)(2,1)S(1)} %get-tuple-element.178), channel_id=1, source_target_pairs={{0,8},{4,12},{24,16},{28,20},{1,9},{5,13},{25,17},{29,21},{2,10},{... | collective-permute-start | bytes 2088968 | tf_op jit(solution)/shard_map/ppermute | solution.py:435
  238.8 21.2 %collective-permute-start.24 = (s16[272,1280]{1,0:T(8,128)(2,1)}, s16[272,1280]{1,0:T(8,128)(2,1)}, u32[]{:S(2)}, u32[]{:S(2)}) collective-permute-start(s16[272,1280]{1,0:T(8,128)(2,1)} %get-tuple-element.174), channel_id=1, source_target_pairs={{8,16},{12,20},{16,8},{20,12},{9,17},{13,21},{17,9},{21,13},{10,18... | collective-permute-start | bytes 2088968 | tf_op jit(solution)/shard_map/ppermute | solution.py:435
  240.5 27.1 %collective-permute-start.29 = (s16[272,1280]{1,0:T(8,128)(2,1)}, s16[272,1280]{1,0:T(8,128)(2,1)}, u32[]{:S(2)}, u32[]{:S(2)}) collective-permute-start(s16[272,1280]{1,0:T(8,128)(2,1)} %get-tuple-element.190), channel_id=1, source_target_pairs={{8,16},{12,20},{16,8},{20,12},{9,17},{13,21},{17,9},{21,13},{10,18... | collective-permute-start | bytes 2088968 | tf_op jit(solution)/shard_map/ppermute | solution.py:435
  249.6 21.6 %collective-permute-start.28 = (s16[272,1280]{1,0:T(8,128)(2,1)}, s16[272,1280]{1,0:T(8,128)(2,1)S(1)}, u32[]{:S(2)}, u32[]{:S(2)}) collective-permute-start(s16[272,1280]{1,0:T(8,128)(2,1)} %get-tuple-element.188), channel_id=1, source_target_pairs={{0,8},{4,12},{24,16},{28,20},{1,9},{5,13},{25,17},{29,21},{2,10},{... | collective-permute-start | bytes 2088968 | tf_op jit(solution)/shard_map/ppermute | solution.py:435
  263.1 24.0 %collective-permute-start.27 = (bf16[256,1280]{1,0:T(8,128)(2,1)S(1)}, bf16[256,1280]{1,0:T(8,128)(2,1)S(1)}, u32[]{:S(2)}, u32[]{:S(2)}) collective-permute-start(bf16[256,1280]{1,0:T(8,128)(2,1)S(1)} %get-tuple-element.186.refs_1_), channel_id=1, source_target_pairs={{0,4},{4,0},{8,12},{12,8},{16,20},{20,16},{24,28},{28,24},{1,5},{5... | collective-permute-start | bytes 1966088 | tf_op jit(solution)/shard_map/ppermute | solution.py:439
  263.2 27.4 %collective-permute-start.32 = (s16[272,1280]{1,0:T(8,128)(2,1)S(1)}, s16[272,1280]{1,0:T(8,128)(2,1)S(1)}, u32[]{:S(2)}, u32[]{:S(2)}) collective-permute-start(s16[272,1280]{1,0:T(8,128)(2,1)S(1)} %get-tuple-element.198), channel_id=1, source_target_pairs={{0,8},{4,12},{24,16},{28,20},{1,9},{5,13},{25,17},{29,21},{2,10},{... | collective-permute-start | bytes 2088968 | tf_op jit(solution)/shard_map/ppermute | solution.py:435
  270.9 21.3 %collective-permute-start.31 = (bf16[256,1280]{1,0:T(8,128)(2,1)S(1)}, bf16[256,1280]{1,0:T(8,128)(2,1)S(1)}, u32[]{:S(2)}, u32[]{:S(2)}) collective-permute-start(bf16[256,1280]{1,0:T(8,128)(2,1)S(1)} %get-tuple-element.196.refs_1_), channel_id=1, source_target_pairs={{0,4},{4,0},{8,12},{12,8},{16,20},{20,16},{24,28},{28,24},{1,5},{5... | collective-permute-start | bytes 1966088 | tf_op jit(solution)/shard_map/ppermute | solution.py:439
  272.1 21.5 %collective-permute-start.34 = (s16[272,1280]{1,0:T(8,128)(2,1)S(1)}, s16[272,1280]{1,0:T(8,128)(2,1)S(1)}, u32[]{:S(2)}, u32[]{:S(2)}) collective-permute-start(s16[272,1280]{1,0:T(8,128)(2,1)S(1)} %get-tuple-element.204), channel_id=1, source_target_pairs={{8,16},{12,20},{16,8},{20,12},{9,17},{13,21},{17,9},{21,13},{10,18... | collective-permute-start | bytes 2088968 | tf_op jit(solution)/shard_map/ppermute | solution.py:435
  273.1 29.0 %collective-permute-start.36 = (s16[272,1280]{1,0:T(8,128)(2,1)S(1)}, s16[272,1280]{1,0:T(8,128)(2,1)S(1)}, u32[]{:S(2)}, u32[]{:S(2)}) collective-permute-start(s16[272,1280]{1,0:T(8,128)(2,1)S(1)} %get-tuple-element.208), channel_id=1, source_target_pairs={{0,8},{4,12},{24,16},{28,20},{1,9},{5,13},{25,17},{29,21},{2,10},{... | collective-permute-start | bytes 2088968 | tf_op jit(solution)/shard_map/ppermute | solution.py:435
  294.2 17.7 %collective-permute-start.30 = (bf16[128,1280]{1,0:T(8,128)(2,1)}, bf16[128,1280]{1,0:T(8,128)(2,1)}, u32[]{:S(2)}, u32[]{:S(2)}) collective-permute-start(bf16[128,1280]{1,0:T(8,128)(2,1)} %get-tuple-element.194), channel_id=1, source_target_pairs={{8,0},{12,4},{16,24},{20,28},{9,1},{13,5},{17,25},{21,29},{10,2},{... | collective-permute-start | bytes 983048 | tf_op jit(solution)/shard_map/ppermute | solution.py:455
  307.5 19.4 %collective-permute-start.33 = (bf16[128,1280]{1,0:T(8,128)(2,1)}, bf16[128,1280]{1,0:T(8,128)(2,1)S(1)}, u32[]{:S(2)}, u32[]{:S(2)}) collective-permute-start(bf16[128,1280]{1,0:T(8,128)(2,1)} %copy-done.34), channel_id=1, source_target_pairs={{8,0},{12,4},{16,24},{20,28},{9,1},{13,5},{17,25},{21,29},{10,2},{... | collective-permute-start | bytes 983048 | tf_op jit(solution)/shard_map/ppermute | solution.py:455
  312.9 20.8 %collective-permute-start.37 = (bf16[128,1280]{1,0:T(8,128)(2,1)}, bf16[128,1280]{1,0:T(8,128)(2,1)S(1)}, u32[]{:S(2)}, u32[]{:S(2)}) collective-permute-start(bf16[128,1280]{1,0:T(8,128)(2,1)} %copy-done.35), channel_id=1, source_target_pairs={{8,0},{12,4},{16,24},{20,28},{9,1},{13,5},{17,25},{21,29},{10,2},{... | collective-permute-start | bytes 983048 | tf_op jit(solution)/shard_map/ppermute | solution.py:455
  (64 other events, 452.9 us)
